TPU v7x, 32 devices: a whole 2x2x4 slice. The times are simulated.
32 devices in a mesh: orb: 2 (over core), box: 16 (over z, y, x).
Axes of the slice: x: 2, y: 2, z: 4, core: 2. Of those that a mesh axis runs over, the one named last changes fastest.
Arguments:
- orbitals: bfloat16 [768, 128, 1000], P('orb', 'box'), may hold values from -6 to 6
- exchange_values: bfloat16 [768, 128, 1000], P('orb', 'box'), may hold values from -6 to 6
- local_values: float32 [128, 1000], P('box'), may hold values from -6 to 6
- coupling: bfloat16 [768, 768], P('orb'), may hold values from -0.21875 to 0.21875
- to_values_mat: float32 [10, 10], replicated, may hold values from -2 to 2
- to_coeffs_mat: float32 [10, 10], replicated, may hold values from -2 to 2
- laplace_blocks: float32 [3, 10, 10], replicated, may hold values from -2 to 2
- box_counts: int32 [16], P('box'), may hold values from 2 to 8, as said below
- kept_mask: int32 [128], P('box'), may hold values from 0 to 1, as said below
- send_list: int32 [16, 16], P('box'), may hold values from -1 to 7, as said below
- neighbour_pos: int32 [6, 128], P(None, 'box'), may hold values from -1 to 23, as said below
Outputs:
- h_orbitals: bfloat16 [768, 128, 1000], P('orb', 'box')
Inputs may be any that keep to these rules, and one draw needn't show every extreme that they name: Device d of box holds live boxes in slots 0 to box_counts[d] - 1 of its 8; some device holds 8. `kept_mask`: 1 only on live boxes; at most 4 ones in one device's range, and exactly 4 in some device's range. `send_list`: row q, entries p * 1 to p + 1 - 1: live slots of device q's range passed to device p, -1 for an empty entry; nothing to its own device; at most 1 to one device, exactly 1 to the devices whose index differs by one. `neighbour_pos`: Boxes that are not live have -1 on every face.
All inputs are finite; a program needn't handle non-finite values.
Results may differ from a plain program's by a relative error of at most 0.0031.
Values may be sent and summed in bfloat16 or wider, within the bound.
A program may use at most 320 MiB of HBM per device.

v0:
```python
import jax
import jax.numpy as jnp
from jax import lax
from jax.sharding import PartitionSpec as P


def along_axis(flat, matrix, which):
    order_k = matrix.shape[0]
    width = flat.shape[-1]
    if which == 0:
        shaped = flat.reshape(-1, order_k, width // order_k)
        result = jnp.einsum("ax,nxr->nar", matrix, shaped, precision=lax.Precision.HIGHEST)
        return result.reshape(flat.shape)
    ident = jnp.eye(order_k, dtype=jnp.float32)
    if which == 1:
        square = jnp.kron(matrix, ident)
    else:
        square = jnp.kron(ident, matrix)
    inner = order_k * order_k
    result = jnp.dot(flat.reshape(-1, inner), square.T, precision=lax.Precision.HIGHEST)
    return result.reshape(flat.shape)


def three_way(flat, matrix):
    order_k = matrix.shape[0]
    inner = order_k * order_k
    first = along_axis(flat, matrix, 0)
    square = jnp.kron(matrix, matrix)
    result = jnp.dot(first.reshape(-1, inner), square.T, precision=lax.Precision.HIGHEST)
    return result.reshape(flat.shape)


def shards(
    orbitals,
    exchange_values,
    local_values,
    coupling,
    to_values_mat,
    to_coeffs_mat,
    laplace_blocks,
    box_counts,
    kept_mask,
    send_list,
    neighbour_pos,
):
    orb_dev, box_dev, width = orbitals.shape
    live = lax.iota(jnp.int32, box_dev) < box_counts[0]
    kept = kept_mask > 0
    slots = send_list[0]
    picked = jnp.take(orbitals, jnp.maximum(slots, 0), axis=1)
    outgoing = jnp.where((slots >= 0)[None, :, None], picked, jnp.zeros_like(picked))
    incoming = lax.all_to_all(outgoing, "box", split_axis=1, concat_axis=1, tiled=True)
    center = orbitals.astype(jnp.float32)
    values = three_way(center, to_values_mat)
    products = jnp.where(
        kept[None, :, None], exchange_values.astype(jnp.float32) * values, 0.0
    ).astype(jnp.bfloat16)
    mixed = jnp.dot(
        coupling,
        lax.all_gather(products.reshape(orb_dev, box_dev * width), "orb", axis=0, tiled=True),
        preferred_element_type=jnp.float32,
    )
    exchange = mixed.reshape(orb_dev, box_dev, width)
    weighted = local_values[None, :, :] * values - exchange
    potential_part = three_way(weighted, to_coeffs_mat)
    pool = jnp.concatenate([orbitals, incoming], axis=1)
    kinetic = jnp.zeros_like(center)
    for which in range(3):
        kinetic = kinetic + along_axis(center, laplace_blocks[0], which)
        for side in range(2):
            face_pos = neighbour_pos[2 * which + side]
            moved = jnp.take(pool, jnp.maximum(face_pos, 0), axis=1)
            moved = jnp.where((face_pos >= 0)[None, :, None], moved, jnp.zeros_like(moved))
            kinetic = kinetic + along_axis(
                moved.astype(jnp.float32), laplace_blocks[1 + side], which
            )
    total = potential_part - 0.5 * kinetic
    total = jnp.where(live[None, :, None], total, 0.0)
    return total.astype(jnp.bfloat16)


def solution(mesh):
    return jax.shard_map(
        shards,
        mesh=mesh,
        in_specs=(
            P("orb", "box", None),
            P("orb", "box", None),
            P("box", None),
            P("orb", None),
            P(),
            P(),
            P(),
            P("box"),
            P("box"),
            P("box", None),
            P(None, "box"),
        ),
        out_specs=P("orb", "box", None),
        check_vma=False,
    )
```

profile of v0, /device:TPU:6, one launch (start us, length us, event | category | flops | bytes accessed | tf_op | source)
XLA Modules:
  0.0 1278.6 jit_solution(9551188158205030759)
XLA Ops:
  17.1 10.9 select_bitcast_fusion
  44.4 21.4 %reshape.298 = bf16[3072,10,100]{2,1,0:T(8,128)(2,1)} reshape(bf16[384,8,1000]{2,1,0:T(8,128)(2,1)} %copy.79) | data formatting | bytes 12288000 | tf_op jit(solution)/shard_map/reshape | solution.py:11
  65.8 17.8 %copy.80 = bf16[3072,10,100]{0,1,2:T(8,128)(2,1)} copy(bf16[3072,10,100]{2,1,0:T(8,128)(2,1)} %reshape.298) | data formatting | bytes 12288000 | tf_op jit(solution)/shard_map/reshape | solution.py:11
  83.6 16.3 %convolution_bitcast_fusion.4 = f32[3072,10,100]{0,1,2:T(8,128)} fusion(bf16[3072,10,100]{0,1,2:T(8,128)(2,1)} %copy.80, f32[10,10]{1,0:T(8,128)S(1)} %copy-done.9), kind=kOutput, calls=%fused_computation.16 | convolution fusion | flops 368640000 | bytes 18432400 | tf_op jit(solution)/shard_map/ax,nxr->nar/dot_general | solution.py:12
  99.9 22.8 %copy.81 = f32[3072,10,100]{2,1,0:T(8,128)} copy(f32[3072,10,100]{0,1,2:T(8,128)} %convolution_bitcast_fusion.4) | data formatting | bytes 24576000 | tf_op jit(solution)/shard_map/ax,nxr->nar/transpose | solution.py:12
  122.8 21.1 %reshape_reshape.6 = f32[30720,100]{1,0:T(8,128)} reshape(f32[3072,10,100]{2,1,0:T(8,128)} %copy.81) | data formatting | bytes 24576000 | tf_op jit(solution)/shard_map/reshape;reshape | solution.py:29
  144.3 17.2 %fusion.6 = f32[30720,100]{1,0:T(8,128)} fusion(f32[30720,100]{1,0:T(8,128)} %reshape_reshape.6, f32[100,100]{1,0:T(8,128)S(1)} %mul.216), kind=kOutput, calls=%fused_computation.76 | convolution fusion | flops 3686400000 | bytes 24616000 | tf_op jit(solution)/shard_map/dot_general | solution.py:29
  161.6 16.6 %reshape.300 = f32[384,8,1000]{2,1,0:T(8,128)} reshape(f32[30720,100]{1,0:T(8,128)} %fusion.6) | data formatting | bytes 24576000 | tf_op jit(solution)/shard_map/reshape | solution.py:30
  178.2 12.8 %copy.84 = f32[384,8,1000]{0,2,1:T(8,128)} copy(f32[384,8,1000]{2,1,0:T(8,128)} %reshape.300) | data formatting | bytes 24576000 | tf_op jit(solution)/shard_map/reshape | solution.py:30
  191.1 10.6 select_convert_fusion.1
  201.6 20.5 %reshape.299 = f32[3072,10,100]{2,1,0:T(8,128)} reshape(f32[30720,100]{1,0:T(8,128)} %fusion.6) | data formatting | bytes 24576000 | tf_op jit(solution)/shard_map/reshape | solution.py:30
  222.2 16.4 %reshape.306 = bf16[30720,100]{1,0:T(8,128)(2,1)} reshape(bf16[384,8,1000]{2,1,0:T(8,128)(2,1)} %copy.79) | data formatting | bytes 12288000 | tf_op jit(solution)/shard_map/reshape | solution.py:20
  244.7 23.6 %mul.212 = f32[3072,10,100]{2,1,0:T(8,128)} reshape(f32[384,8,1000]{2,1,0:T(8,128)} %mul.211) | data formatting | bytes 24576000 | tf_op jit(solution)/shard_map/mul | solution.py:64
  277.1 12.1 convolution_bitcast_fusion
  289.2 14.6 %copy.108 = f32[30720,100]{1,0:T(8,128)} copy(f32[30720,100]{0,1:T(8,128)} %convolution_bitcast_fusion) | data formatting | bytes 24576000 | tf_op jit(solution)/shard_map/dot_general | solution.py:20
  303.8 16.6 %reshape.312 = f32[384,8,1000]{2,1,0:T(8,128)} reshape(f32[30720,100]{1,0:T(8,128)} %copy.108) | data formatting | bytes 24576000 | tf_op jit(solution)/shard_map/reshape | solution.py:21
  320.4 12.6 copy.109
  335.0 23.1 %convolution_bitcast_fusion.1 = f32[30720,100]{0,1:T(8,128)} fusion(f32[100,100]{1,0:T(8,128)S(1)} %mul.226, bf16[30720,100]{1,0:T(8,128)(2,1)} %reshape.306), kind=kOutput, calls=%fused_computation.8 | convolution fusion | flops 3686400000 | bytes 18472000 | tf_op jit(solution)/shard_map/dot_general | solution.py:20
  358.1 14.6 %copy.99 = f32[30720,100]{1,0:T(8,128)} copy(f32[30720,100]{0,1:T(8,128)} %convolution_bitcast_fusion.1) | data formatting | bytes 24576000 | tf_op jit(solution)/shard_map/dot_general | solution.py:20
  372.7 16.6 %reshape.307 = f32[384,8,1000]{2,1,0:T(8,128)} reshape(f32[30720,100]{1,0:T(8,128)} %copy.99) | data formatting | bytes 24576000 | tf_op jit(solution)/shard_map/reshape | solution.py:21
  389.3 12.6 copy.101
  412.1 16.3 %fusion = f32[3072,100,10]{0,2,1:T(8,128)} fusion(bf16[3072,10,100]{0,1,2:T(8,128)(2,1)} %copy.80, f32[1,10,10]{2,0,1:T(1,128)S(1)} %get-tuple-element.18), kind=kOutput, calls=%fused_computation.37 | convolution fusion | flops 368640000 | bytes 18432400 | tf_op jit(solution)/shard_map/ax,nxr->nar/dot_general | solution.py:12
  428.4 12.0 convolution_bitcast_fusion.2
  440.4 12.6 copy.85
  453.0 24.1 %reshape.302 = f32[3072,10,100]{2,1,0:T(8,128)} reshape(f32[384,8000]{1,0:T(8,128)} %copy.85) | data formatting | bytes 24576000 | tf_op jit(solution)/shard_map/reshape | solution.py:63
  477.1 33.0 %multiply_subtract_fusion = f32[3072,10,100]{2,1,0:T(8,128)} fusion(f32[3072,10,100]{2,1,0:T(8,128)} %reshape.302, f32[3072,10,100]{2,1,0:T(8,128)} %mul.212, f32[3072,10,100]{2,1,0:T(8,128)} %reshape.299), kind=kLoop, calls=%fused_computation.9 | loop fusion | flops 6144000 | bytes 49152000 | tf_op jit(solution)/shard_map/sub | solution.py:64
  510.1 23.4 %copy.86 = f32[3072,10,100]{0,1,2:T(8,128)} copy(f32[3072,10,100]{2,1,0:T(8,128)} %multiply_subtract_fusion) | data formatting | bytes 24576000 | tf_op jit(solution)/shard_map/sub | solution.py:64
  533.5 35.0 %convolution_bitcast_fusion.3 = f32[3072,10,100]{0,1,2:T(8,128)} fusion(f32[3072,10,100]{0,1,2:T(8,128)} %copy.86, f32[10,10]{1,0:T(8,128)S(1)} %copy-done.8), kind=kOutput, calls=%fused_computation.15 | convolution fusion | flops 368640000 | bytes 24576400 | tf_op jit(solution)/shard_map/ax,nxr->nar/dot_general | solution.py:12
  568.5 22.8 %copy.87 = f32[3072,10,100]{2,1,0:T(8,128)} copy(f32[3072,10,100]{0,1,2:T(8,128)} %convolution_bitcast_fusion.3) | data formatting | bytes 24576000 | tf_op jit(solution)/shard_map/ax,nxr->nar/transpose | solution.py:12
  591.4 21.1 %reshape_reshape.7 = f32[30720,100]{1,0:T(8,128)} reshape(f32[3072,10,100]{2,1,0:T(8,128)} %copy.87) | data formatting | bytes 24576000 | tf_op jit(solution)/shard_map/reshape;reshape | solution.py:29
  612.5 17.3 %fusion.7 = f32[30720,100]{1,0:T(8,128)} fusion(f32[30720,100]{1,0:T(8,128)} %reshape_reshape.7, f32[100,100]{1,0:T(8,128)S(1)} %copy-done.2), kind=kOutput, calls=%fused_computation.77 | convolution fusion | flops 3686400000 | bytes 24616000 | tf_op jit(solution)/shard_map/dot_general | solution.py:29
  629.8 16.6 %reshape.303 = f32[384,8,1000]{2,1,0:T(8,128)} reshape(f32[30720,100]{1,0:T(8,128)} %fusion.7) | data formatting | bytes 24576000 | tf_op jit(solution)/shard_map/reshape | solution.py:30
  646.4 12.6 copy.116
  695.4 16.4 %reshape.315 = bf16[30720,100]{1,0:T(8,128)(2,1)} reshape(bf16[384,8,1000]{2,1,0:T(8,128)(2,1)} %copy.113) | data formatting | bytes 12288000 | tf_op jit(solution)/shard_map/reshape | solution.py:20
  711.8 12.1 fusion.11
  723.9 16.6 %reshape.316 = f32[384,8,1000]{2,1,0:T(8,128)} reshape(f32[30720,100]{1,0:T(8,128)} %fusion.11) | data formatting | bytes 24576000 | tf_op jit(solution)/shard_map/reshape | solution.py:21
  740.5 12.6 copy.115
  753.1 10.5 gather_fusion.5
  778.9 16.4 %reshape.313 = bf16[30720,100]{1,0:T(8,128)(2,1)} reshape(bf16[384,8,1000]{2,1,0:T(8,128)(2,1)} %copy.110) | data formatting | bytes 12288000 | tf_op jit(solution)/shard_map/reshape | solution.py:20
  795.3 12.3 fusion.10
  807.6 16.6 %reshape.314 = f32[384,8,1000]{2,1,0:T(8,128)} reshape(f32[30720,100]{1,0:T(8,128)} %fusion.10) | data formatting | bytes 24576000 | tf_op jit(solution)/shard_map/reshape | solution.py:21
  824.2 12.6 copy.112
  836.8 10.5 gather_fusion.4
  862.7 16.4 %reshape.310 = bf16[30720,100]{1,0:T(8,128)(2,1)} reshape(bf16[384,8,1000]{2,1,0:T(8,128)(2,1)} %copy.105) | data formatting | bytes 12288000 | tf_op jit(solution)/shard_map/reshape | solution.py:20
  879.1 12.1 fusion.9
  891.2 16.6 %reshape.311 = f32[384,8,1000]{2,1,0:T(8,128)} reshape(f32[30720,100]{1,0:T(8,128)} %fusion.9) | data formatting | bytes 24576000 | tf_op jit(solution)/shard_map/reshape | solution.py:21
  907.8 12.9 %copy.107 = f32[384,8,1000]{0,2,1:T(8,128)} copy(f32[384,8,1000]{2,1,0:T(8,128)} %reshape.311) | data formatting | bytes 24576000 | tf_op jit(solution)/shard_map/reshape | solution.py:21
  920.8 10.5 gather_fusion.3
  946.5 16.4 %reshape.308 = bf16[30720,100]{1,0:T(8,128)(2,1)} reshape(bf16[384,8,1000]{2,1,0:T(8,128)(2,1)} %copy.102) | data formatting | bytes 12288000 | tf_op jit(solution)/shard_map/reshape | solution.py:20
  963.0 12.1 fusion.8
  975.1 16.6 %reshape.309 = f32[384,8,1000]{2,1,0:T(8,128)} reshape(f32[30720,100]{1,0:T(8,128)} %fusion.8) | data formatting | bytes 24576000 | tf_op jit(solution)/shard_map/reshape | solution.py:21
  991.7 12.6 copy.104
  1004.3 10.5 gather_fusion.1
  1030.1 21.4 %reshape.304 = bf16[3072,10,100]{2,1,0:T(8,128)(2,1)} reshape(bf16[384,8,1000]{2,1,0:T(8,128)(2,1)} %copy.91) | data formatting | bytes 12288000 | tf_op jit(solution)/shard_map/reshape | solution.py:11
  1051.6 17.9 %copy.93 = bf16[3072,10,100]{0,1,2:T(8,128)(2,1)} copy(bf16[3072,10,100]{2,1,0:T(8,128)(2,1)} %reshape.304) | data formatting | bytes 12288000 | tf_op jit(solution)/shard_map/reshape | solution.py:11
  1069.4 16.5 %fusion.1 = f32[3072,100,10]{0,2,1:T(8,128)} fusion(bf16[3072,10,100]{0,1,2:T(8,128)(2,1)} %copy.93, f32[1,10,10]{2,0,1:T(1,128)S(1)} %copy-done.13), kind=kOutput, calls=%fused_computation.38 | convolution fusion | flops 368640000 | bytes 18432400 | tf_op jit(solution)/shard_map/ax,nxr->nar/dot_general | solution.py:12
  1085.9 10.5 gather_fusion.2
  1111.8 21.4 %reshape.305 = bf16[3072,10,100]{2,1,0:T(8,128)(2,1)} reshape(bf16[384,8,1000]{2,1,0:T(8,128)(2,1)} %copy.94) | data formatting | bytes 12288000 | tf_op jit(solution)/shard_map/reshape | solution.py:11
  1133.2 17.8 %copy.96 = bf16[3072,10,100]{0,1,2:T(8,128)(2,1)} copy(bf16[3072,10,100]{2,1,0:T(8,128)(2,1)} %reshape.305) | data formatting | bytes 12288000 | tf_op jit(solution)/shard_map/reshape | solution.py:11
  1151.0 30.2 %add_bitcast_fusion = f32[3072,10,100]{0,1,2:T(8,128)} fusion(f32[3072,100,10]{0,2,1:T(8,128)} %fusion, f32[3072,100,10]{0,2,1:T(8,128)} %fusion.1, bf16[3072,10,100]{0,1,2:T(8,128)(2,1)} %copy.96, f32[1,10,10]{2,0,1:T(1,128)S(1)} %copy-done.11), kind=kOutput, calls=%fused_computation.10 | convolution fusion | flops 374784000 | bytes 43008400 | tf_op jit(solution)/shard_map/ax,nxr->nar/dot_general | solution.py:12
  1181.2 22.8 %copy.97 = f32[3072,10,100]{2,1,0:T(8,128)} copy(f32[3072,10,100]{0,1,2:T(8,128)} %add_bitcast_fusion) | data formatting | bytes 24576000 | tf_op jit(solution)/shard_map/add | solution.py:74
  1204.1 21.6 %add.40 = f32[384,8,1000]{2,1,0:T(8,128)} reshape(f32[3072,10,100]{2,1,0:T(8,128)} %copy.97) | data formatting | bytes 24576000 | tf_op jit(solution)/shard_map/add | solution.py:74
  1225.7 12.6 copy.100
  1238.3 33.2 %select_convert_fusion = bf16[384,8,1000]{0,2,1:T(8,128)(2,1)} fusion(f32[384,8,1000]{0,2,1:T(8,128)} %copy.116, f32[384,8,1000]{0,2,1:T(8,128)} %copy.115, f32[384,8,1000]{0,2,1:T(8,128)} %copy.112, f32[384,8,1000]{0,2,1:T(8,128)} %copy.109, f32[384,8,1000]{0,2,1:T(8,128)} %copy.107, f32[384,8,1000]{0,2,1:T(8,128)} %copy.104, f32[384,8,1000]{0,2,1:T(8,128)} %copy.100, ...), kind=kLoop, calls=%fused_computation.12 | loop fusion | flops 30720000 | bytes 104448008 | tf_op jit(solution)/shard_map/convert_element_type | solution.py:79
  (110 shorter events, 166.7 us)
Async XLA Ops:
  6.5 421.8 %copy-start = (bf16[384,768]{1,0:T(8,128)(2,1)S(1)}, bf16[384,768]{1,0:T(8,128)(2,1)}, u32[]{:S(2)}) copy-start(bf16[384,768]{1,0:T(8,128)(2,1)} %param.16) | copy-start | bytes 1769476
  27.9 631.0 %all-to-all-start = ((bf16[384,16,1000]{0,2,1:T(8,128)(2,1)}), bf16[384,16,1000]{0,2,1:T(8,128)(2,1)}, u32[]{:S(2)}, u32[]{:S(2)}) async-start(bf16[384,16,1000]{0,2,1:T(8,128)(2,1)} %select_bitcast_fusion), calls=%async_computation | async-start | bytes 24576000 | tf_op jit(solution)/shard_map/all_to_all | solution.py:52
  35.3 393.1 %all-gather.2.cloned.1.call-start = ((), (), s32[]{:S(2)}) async-start(), calls=%async_computation.1 | async-start | bytes 18432000 | tf_op jit(solution)/shard_map/all_gather | solution.py:60
  65.8 17.8 %copy-start.9 = (f32[10,10]{1,0:T(8,128)S(1)}, f32[10,10]{1,0:T(8,128)}, u32[]{:S(2)}) copy-start(f32[10,10]{1,0:T(8,128)} %param.17) | copy-start | bytes 1204
  178.2 12.8 %copy-start.30 = (s32[8]{0:T(128)S(1)}, s32[8]{0:T(128)}, u32[]{:S(2)}) copy-start(s32[8]{0:T(128)} %param.21) | copy-start | bytes 100
  222.2 16.4 %copy-start.14 = (f32[8,1000]{1,0:T(8,128)S(1)}, f32[8,1000]{1,0:T(8,128)}, u32[]{:S(2)}) copy-start(f32[8,1000]{1,0:T(8,128)} %param.15) | copy-start | bytes 96004
  244.7 23.6 %copy-start.7 = (f32[10,10]{1,0:T(8,128)S(1)}, f32[10,10]{1,0:T(8,128)}, u32[]{:S(2)}) copy-start(f32[10,10]{1,0:T(8,128)} %param.18) | copy-start | bytes 1204
  244.7 24.6 %copy-start.15 = (f32[3,10,10]{2,0,1:T(4,128)S(1)}, f32[3,10,10]{2,0,1:T(4,128)}, u32[]{:S(2)}) copy-start(f32[3,10,10]{2,0,1:T(4,128)} %param.19) | copy-start | bytes 3604
  269.3 0.6 copy-start.10
  269.3 0.6 copy-start.12
  389.3 13.7 %copy-start.16 = (s32[6,8]{1,0:T(8,128)S(1)}, s32[6,8]{1,0:T(8,128)}, u32[]{:S(2)}) copy-start(s32[6,8]{1,0:T(8,128)} %param.23) | copy-start | bytes 580
  510.1 23.4 %copy-start.8 = (f32[10,10]{1,0:T(8,128)S(1)}, f32[10,10]{1,0:T(8,128)}, u32[]{:S(2)}) copy-start(f32[10,10]{1,0:T(8,128)} %param.18) | copy-start | bytes 1204
  591.4 21.1 %copy-start.2 = (f32[100,100]{1,0:T(8,128)S(1)}, f32[100,100]{1,0:T(8,128)}, u32[]{:S(2)}) copy-start(f32[100,100]{1,0:T(8,128)} %mul.222) | copy-start | bytes 120004
  669.4 10.5 copy-start.26
  669.4 10.5 copy-start.28
  686.3 25.5 %copy-start.6 = (f32[100,100]{1,0:T(8,128)S(1)}, f32[100,100]{1,0:T(8,128)}, u32[]{:S(2)}) copy-start(f32[100,100]{1,0:T(8,128)} %mul.242) | copy-start | bytes 120004
  753.1 10.5 copy-start.24
  753.1 10.5 copy-start.27
  769.9 25.4 %copy-start.5 = (f32[100,100]{1,0:T(8,128)S(1)}, f32[100,100]{1,0:T(8,128)}, u32[]{:S(2)}) copy-start(f32[100,100]{1,0:T(8,128)} %mul.239) | copy-start | bytes 120004
  836.8 10.5 copy-start.22
  836.8 10.5 copy-start.25
  853.6 25.5 %copy-start.4 = (f32[100,100]{1,0:T(8,128)S(1)}, f32[100,100]{1,0:T(8,128)}, u32[]{:S(2)}) copy-start(f32[100,100]{1,0:T(8,128)} %mul.232) | copy-start | bytes 120004
  920.7 10.5 copy-start.20
  920.7 10.5 copy-start.23
  937.6 25.4 %copy-start.3 = (f32[100,100]{1,0:T(8,128)S(1)}, f32[100,100]{1,0:T(8,128)}, u32[]{:S(2)}) copy-start(f32[100,100]{1,0:T(8,128)} %mul.229) | copy-start | bytes 120004
  1004.3 10.5 copy-start.18
  1004.3 10.5 copy-start.21
  1051.5 17.9 %copy-start.13 = (f32[1,10,10]{2,0,1:T(1,128)S(1)}, f32[1,10,10]{2,0,1:T(1,128)}, u32[]{:S(2)}) copy-start(f32[1,10,10]{2,0,1:T(1,128)} %copy-done.12) | copy-start | bytes 1204
  1085.9 10.5 copy-start.17
  1085.9 10.5 copy-start.19
  1133.2 17.9 %copy-start.11 = (f32[1,10,10]{2,0,1:T(1,128)S(1)}, f32[1,10,10]{2,0,1:T(1,128)}, u32[]{:S(2)}) copy-start(f32[1,10,10]{2,0,1:T(1,128)} %copy-done.10) | copy-start | bytes 1204
  1225.7 12.6 copy-start.29
  1238.3 33.2 %copy-start.1 = (bf16[384,768]{1,0:T(8,128)(2,1)S(1)}, bf16[384,768]{1,0:T(8,128)(2,1)}, u32[]{:S(2)}) copy-start(bf16[384,768]{1,0:T(8,128)(2,1)} %param.16) | copy-start | bytes 1769476
Sparse Core Ops, SparseCore 0:
  201.8 25.7 all-gather.1
where the time goes:
time: 1300 us; the launch traced here: 1280 us
  local copies, waits for them, and re-layouts  879 us (68%)
  matrix products  245 us (19%)
  other arithmetic  133 us (10%)
  between operations  14.5 us (1%)
    reshape x12, local copies, waits for them, and re-layouts, along_axis(): return result.reshape(flat.shape)  175 us
    reshape x6, local copies, waits for them, and re-layouts, along_axis(): shaped = flat.reshape(-1, order_k, width // order_k)  118 us
    dot_general x5, matrix products, along_axis(): jnp.einsum('ax,nxr->nar', matrix, shaped, precision=lax.Precision.HIGHEST)  114 us
    dot_general x6, matrix products, along_axis(): jnp.dot(flat.reshape(-1, inner), square.T, precision=lax.Precision.HIGHEST)  83.8 us
    reshape x5, local copies, waits for them, and re-layouts, along_axis(): flat.reshape(-1, inner)  82.1 us
    reshape x5, local copies, waits for them, and re-layouts, three_way(): return result.reshape(flat.shape)  79.2 us
    gather x6, local copies, waits for them, and re-layouts, shards(): moved = jnp.take(pool, jnp.maximum(face_pos, 0), axis=1)  63 us
    add x3, local copies, waits for them, and re-layouts, shards(): kinetic + along_axis(moved.astype(jnp.float32), laplace_blocks[1 + side],...  57.1 us
  transfers between devices with their start and end apart: 2, of which 0 were waited for; matrix products, arithmetic and copies ran while one was open for 49% of the time, Pallas kernels for 0%

commit v1 on v0

v1 whole, which is shorter than its diff:
```python
import functools

import jax
import jax.numpy as jnp
from jax import lax
from jax.experimental import pallas as pl
from jax.experimental.pallas import tpu as pltpu
from jax.sharding import PartitionSpec as P

F32, BF16 = jnp.float32, jnp.bfloat16


def split(matrix):
    high = lax.reduce_precision(matrix, 8, 7)
    return high.astype(BF16), (matrix - high).astype(BF16)


def pack_kernel(slots, pool, out, sems):
    def copy(p):
        slot = jnp.maximum(slots[p], 0)
        return pltpu.make_async_copy(pool.at[slot], out.at[p], sems.at[p])

    @pl.loop(0, out.shape[0])
    def _(p):
        copy(p).start()

    @pl.loop(0, out.shape[0])
    def _(p):
        copy(p).wait()


def pack(slots, pool):
    count = slots.shape[0]
    return pl.pallas_call(
        pack_kernel,
        out_shape=jax.ShapeDtypeStruct((count,) + pool.shape[1:], pool.dtype),
        grid_spec=pltpu.PrefetchScalarGridSpec(
            num_scalar_prefetch=1,
            grid=(1,),
            in_specs=[pl.BlockSpec(memory_space=pl.ANY)],
            out_specs=pl.BlockSpec(memory_space=pl.ANY),
            scratch_shapes=[pltpu.SemaphoreType.DMA((count,))],
        ),
    )(slots, pool)


def faces_kernel(faces, count, own, come, part, far, near, out, pool, acc, sems):
    box_dev = own.shape[0]
    total = box_dev + come.shape[0]
    g = pl.program_id(0)

    def copy(n, ref, at):
        return pltpu.make_async_copy(ref.at[n], pool.at[at + n], sems.at[at + n])

    @pl.when(g == 0)
    def _():
        @pl.loop(0, box_dev)
        def _(n):
            copy(n, own, 0).start()

        @pl.loop(0, total - box_dev)
        def _(n):
            copy(n, come, box_dev).start()

        @pl.loop(0, box_dev)
        def _(n):
            copy(n, own, 0).wait()

        @pl.loop(0, total - box_dev)
        def _(n):
            copy(n, come, box_dev).wait()

    @pl.when(g >= count[0])
    def _():
        out[...] = jnp.zeros_like(out)

    @pl.when(g < count[0])
    def _():
        acc[...] = part[0]
        for f in range(6):
            at = faces[f, g]

            @pl.when(at >= 0)
            def _(f=f, at=at):
                x = pool[jnp.maximum(at, 0)]
                if f < 2:
                    acc[...] += jnp.dot(far[f, 0], x, preferred_element_type=F32) + jnp.dot(
                        far[f, 1], x, preferred_element_type=F32
                    )
                else:
                    size = near.shape[-1]
                    for j in range(x.shape[0] // size):
                        rows = pl.ds(j * size, size)
                        y = x[j * size : (j + 1) * size]
                        acc[rows, :] += jnp.dot(
                            near[f - 2, 0], y, preferred_element_type=F32
                        ) + jnp.dot(near[f - 2, 1], y, preferred_element_type=F32)

        out[0] = acc[...].astype(out.dtype)


def apply_faces(faces, count, own, come, part, far, near):
    boxes, width, orbs = own.shape
    total = boxes + come.shape[0]
    full = lambda a: pl.BlockSpec(a.shape, lambda g, *_: (0,) * a.ndim)
    block = pl.BlockSpec((1, width, orbs), lambda g, *_: (g, 0, 0))
    return pl.pallas_call(
        faces_kernel,
        out_shape=jax.ShapeDtypeStruct(own.shape, own.dtype),
        grid_spec=pltpu.PrefetchScalarGridSpec(
            num_scalar_prefetch=2,
            grid=(boxes,),
            in_specs=[
                pl.BlockSpec(memory_space=pl.ANY),
                pl.BlockSpec(memory_space=pl.ANY),
                block,
                full(far),
                full(near),
            ],
            out_specs=block,
            scratch_shapes=[
                pltpu.VMEM((total, width, orbs), own.dtype),
                pltpu.VMEM((width, orbs), F32),
                pltpu.SemaphoreType.DMA((total,)),
            ],
        ),
        compiler_params=pltpu.CompilerParams(vmem_limit_bytes=58 * 2**20),
    )(faces, count, own, come, part, far, near)


def shards(
    orbitals,
    exchange_values,
    local_values,
    coupling,
    to_values_mat,
    to_coeffs_mat,
    laplace_blocks,
    box_counts,
    kept_mask,
    send_list,
    neighbour_pos,
):
    k = to_values_mat.shape[0]
    fields = orbitals.transpose(1, 2, 0)
    exchange_fields = exchange_values.transpose(1, 2, 0)
    outgoing = pack(send_list[0], fields)
    incoming = lax.all_to_all(outgoing, "box", split_axis=0, concat_axis=0, tiled=True)

    apply = functools.partial(jnp.einsum, "ij,bjn->bin", preferred_element_type=F32)
    eye1, eye2 = jnp.eye(k, dtype=F32), jnp.eye(k * k, dtype=F32)
    cube = lambda m: jnp.kron(jnp.kron(m, m), m)
    high, low = split(cube(to_values_mat))
    values = apply(high, fields) + apply(low, fields)
    kept = (kept_mask > 0)[:, None, None]
    products = jnp.where(kept, exchange_fields.astype(F32) * values, 0.0).astype(BF16)
    gathered = lax.all_gather(products, "orb", axis=2, tiled=True)
    exchange = jnp.einsum("bcj,ij->bci", gathered, coupling, preferred_element_type=F32)
    weighted = local_values[:, :, None] * values - exchange
    high, low = split(cube(to_coeffs_mat))
    whigh = lax.reduce_precision(weighted, 8, 7)
    wlow = (weighted - whigh).astype(BF16)
    whigh = whigh.astype(BF16)
    part = apply(high, whigh) + apply(high, wlow) + apply(low, whigh)

    half = -0.5 * laplace_blocks
    own = half[0]
    center = (
        jnp.kron(own, eye2) + jnp.kron(jnp.kron(eye1, own), eye1) + jnp.kron(eye2, own)
    )
    high, low = split(center)
    part = part + apply(high, fields) + apply(low, fields)

    pair = jnp.eye(2, dtype=F32)
    far = jnp.stack([jnp.stack(split(jnp.kron(half[1 + s], eye2))) for s in range(2)])
    near = jnp.stack(
        [
            jnp.stack(split(jnp.kron(pair, m)))
            for m in (
                jnp.kron(half[1], eye1),
                jnp.kron(half[2], eye1),
                jnp.kron(eye1, half[1]),
                jnp.kron(eye1, half[2]),
            )
        ]
    )
    out = apply_faces(neighbour_pos, box_counts, fields, incoming, part, far, near)
    return out.transpose(2, 0, 1)


def solution(mesh):
    return jax.shard_map(
        shards,
        mesh=mesh,
        in_specs=(
            P("orb", "box", None),
            P("orb", "box", None),
            P("box", None),
            P("orb", None),
            P(),
            P(),
            P(),
            P("box"),
            P("box"),
            P("box", None),
            P(None, "box"),
        ),
        out_specs=P("orb", "box", None),
        check_vma=False,
    )
```

time: 1300 us -> 859 us (0.66)
  local copies, waits for them, and re-layouts: 879 us -> 155 us
  Pallas kernels: 0 us -> 448 us
  matrix products: 245 us -> 125 us
  other arithmetic: 133 us -> 99.9 us
    reshape x29 -> x0, local copies, waits for them, and re-layouts: 479 us -> none  [the longest x12 175 us: along_axis(): return result.reshape(flat.shape)]
    pallas_call x0 -> x2, Pallas kernels: none -> 448 us  [the longest x1 374 us: pack(): pl.pallas_call(pack_kernel, out_shape=jax.ShapeDtypeStruct((count,) + poo...]
    dot_general x14 -> x8, matrix products: 245 us -> 125 us  [the longest x2 43.4 us: shards(): part = part + apply(high, fields) + apply(low, fields)]
    mul x10 -> x19, local copies, waits for them, and re-layouts: 38.2 us -> 153 us  [the longest x4 63 us: shards(): cube = lambda m: jnp.kron(jnp.kron(m, m), m)]
    mul x3 -> x10, other arithmetic: 1.99 us -> 85.2 us  [the longest x4 34.9 us: shards(): cube = lambda m: jnp.kron(jnp.kron(m, m), m)]
    gather x7 -> x0, local copies, waits for them, and re-layouts: 72.2 us -> none  [the longest x6 63 us: shards(): moved = jnp.take(pool, jnp.maximum(face_pos, 0), axis=1)]
    add x3 -> x0, local copies, waits for them, and re-layouts: 57.1 us -> none  [shards(): kinetic + along_axis(moved.astype(jnp.float32), laplace_blocks[1 + side],...]
    select_n x6 -> x0, local copies, waits for them, and re-layouts: 54 us -> none  [shards(): jnp.where((face_pos >= 0)[None, :, None], moved, jnp.zeros_like(moved))]
  transfers between devices with their start and end apart: 2 -> 2, of which waited for: 0 -> 0; matrix products, arithmetic and copies ran while one was open for 49% -> 44% of each run, Pallas kernels for 0% -> 0%
where the time goes in v1:
time: 859 us; the launch traced here: 850 us
  Pallas kernels  448 us (52%)
  local copies, waits for them, and re-layouts  155 us (18%)
  matrix products  125 us (15%)
  other arithmetic  99.9 us (12%)
  between operations  14.7 us (2%)
    pallas_call x1, Pallas kernels, pack(): pl.pallas_call(pack_kernel, out_shape=jax.ShapeDtypeStruct((count,) + poo...  374 us
    pallas_call x1, Pallas kernels, apply_faces(): pl.pallas_call(faces_kernel, out_shape=jax.ShapeDtypeStruct(own.shape, ow...  73.8 us
    mul x4, local copies, waits for them, and re-layouts, shards(): cube = lambda m: jnp.kron(jnp.kron(m, m), m)  63 us
    dot_general x2, matrix products, shards(): part = part + apply(high, fields) + apply(low, fields)  43.4 us
    mul x4, other arithmetic, shards(): cube = lambda m: jnp.kron(jnp.kron(m, m), m)  34.9 us
    dot_general x3, matrix products, shards(): part = apply(high, whigh) + apply(high, wlow) + apply(low, whigh)  32.5 us
    mul x1, local copies, waits for them, and re-layouts, shards(): jnp.kron(jnp.kron(eye1, own), eye1)  31.2 us
    mul x1, local copies, waits for them, and re-layouts, shards(): jnp.kron(eye2, own)  31.2 us
  transfers between devices with their start and end apart: 2, of which 0 were waited for; matrix products, arithmetic and copies ran while one was open for 44% of the time, Pallas kernels for 0%

profile of v1, /device:TPU:6, one launch (start us, length us, event | category | flops | bytes accessed | tf_op | source)
XLA Modules:
  0.0 849.6 jit_solution(13473426856119349647)
XLA Ops:
  6.5 0.0 copy-start
  6.5 374.3 %shard_map.109 = bf16[16,1000,384]{2,1,0:T(8,128)(2,1)} custom-call(s32[16]{0:T(128)} %bitcast.79, bf16[8,1000,384]{2,1,0:T(8,128)(2,1)} %bitcast.75), custom_call_target="tpu_custom_call" | custom-call | tf_op jit(solution)/shard_map/pallas_call | solution.py:34
  380.8 0.0 copy-start.10
  380.8 0.0 copy-start.7
  380.9 7.3 all-to-all-start
  388.1 0.0 all-gather.2.cloned.1.call-start
  388.2 0.0 copy-done.10
  388.2 0.0 copy-done.7
  388.2 0.1 broadcast_multiply_fusion.13
  388.3 0.3 mul.448
  388.6 17.4 %broadcast_multiply_fusion.3 = f32[100,10,100,10]{3,2,1,0:T(8,128)} fusion(f32[10,10]{1,0:T(8,128)S(1)} %copy-done.7, f32[100,100]{1,0:T(8,128)S(1)} %mul.448), kind=kLoop, calls=%fused_computation.3 | loop fusion | flops 1000000 | bytes 4040400 | tf_op jit(solution)/shard_map/jit(kron)/mul | solution.py:152
  406.0 31.2 %mul.452 = f32[1000,1000]{1,0:T(8,128)} reshape(f32[100,10,100,10]{3,2,1,0:T(8,128)} %broadcast_multiply_fusion.3) | data formatting | bytes 8000000 | tf_op jit(solution)/shard_map/jit(kron)/mul | solution.py:152
  437.2 13.2 %fusion.18 = f32[1000,8,384]{2,0,1:T(8,128)} fusion(f32[1000,1000]{1,0:T(8,128)} %mul.452, bf16[384,8,1000]{0,2,1:T(8,128)(2,1)} %param.11), kind=kOutput, calls=%fused_computation.42 | convolution fusion | flops 6146999808 | bytes 22432000 | tf_op jit(solution)/shard_map/ij,bjn->bin/dot_general | solution.py:154
  450.4 0.0 copy-done.5
  450.4 16.0 %fusion.2 = (bf16[8,1000,384]{2,1,0:T(8,128)(2,1)}, f32[1000,8,384]{2,0,1:T(8,128)}) fusion(bf16[384,8,1000]{0,2,1:T(8,128)(2,1)} %param.12, pred[8]{0:T(512)(128)(4,1)S(1)} %broadcast_compare_fusion, f32[1000,8,384]{2,0,1:T(8,128)} %fusion.18, bf16[384,8,1000]{0,2,1:T(8,128)(2,1)} %param.11, f32[1000,1000]{1,0:T(8,128)S(1)} %copy-done.5), kind=kOutput, calls=%fused_computation.11 | convolution fusion | flops 6161359872 | bytes 47008008 | tf_op jit(solution)/shard_map/ij,bjn->bin/dot_general | solution.py:154
  466.4 0.0 all-gather.2.cloned.1.call-update
  467.1 0.0 copy-done.9
  467.2 0.0 copy-done.8
  467.2 0.1 broadcast_multiply_fusion.12
  467.3 0.3 mul.458
  467.6 1.4 broadcast_multiply_fusion.10
  469.0 1.4 mul.494
  470.4 1.4 mul.506
  471.7 0.3 mul.512
  472.0 0.3 mul.500
  472.3 0.3 mul.473
  472.5 0.3 broadcast_multiply_fusion.17
  472.8 0.2 mul.497
  473.0 0.2 mul.503
  473.1 0.2 mul.509
  473.3 0.2 mul.515
  473.5 13.9 %broadcast_multiply_fusion.5 = (f32[10,100,10,100]{3,2,1,0:T(8,128)}, f32[10,100,10,100]{3,2,1,0:T(8,128)}, f32[10,100,10,100]{3,2,1,0:T(8,128)}) fusion(f32[10,10]{1,0:T(8,128)S(1)} %get-tuple-element.20, f32[100,100]{1,0:T(8,128)S(1)} %fusion.34, f32[10,10]{1,0:T(8,128)S(1)} %get-tuple-element.21, f32[10,10]{1,0:T(8,128)S(1)} %get-tuple-element.22), kind=kLoop, calls=%fused_computation.34 | loop fusion | flops 3000000 | bytes 12041200 | tf_op jit(solution)/shard_map/jit(kron)/mul | solution.py:175
  487.4 7.7 mul.485
  495.0 7.6 mul.469
  502.7 7.8 mul.489
  510.4 17.3 %broadcast_multiply_fusion = f32[100,10,100,10]{3,2,1,0:T(8,128)} fusion(f32[10,10]{1,0:T(8,128)S(1)} %get-tuple-element.22, f32[100,100]{1,0:T(8,128)S(1)} %fusion.34), kind=kLoop, calls=%fused_computation | loop fusion | flops 1000000 | bytes 4040400 | tf_op jit(solution)/shard_map/jit(kron)/mul | solution.py:169
  527.7 31.2 %mul.481 = f32[1000,1000]{1,0:T(8,128)} reshape(f32[100,10,100,10]{3,2,1,0:T(8,128)} %broadcast_multiply_fusion) | data formatting | bytes 8000000 | tf_op jit(solution)/shard_map/jit(kron)/mul | solution.py:169
  559.0 17.3 %broadcast_multiply_fusion.1 = f32[100,10,100,10]{3,2,1,0:T(8,128)} fusion(f32[10,10]{1,0:T(8,128)S(1)} %fusion.35, f32[100,100]{1,0:T(8,128)S(1)} %mul.473), kind=kLoop, calls=%fused_computation.1 | loop fusion | flops 1000000 | bytes 4040400 | tf_op jit(solution)/shard_map/jit(kron)/mul | solution.py:169
  576.2 31.2 %mul.477 = f32[1000,1000]{1,0:T(8,128)} reshape(f32[100,10,100,10]{3,2,1,0:T(8,128)} %broadcast_multiply_fusion.1) | data formatting | bytes 8000000 | tf_op jit(solution)/shard_map/jit(kron)/mul | solution.py:169
  607.5 17.3 %broadcast_multiply_fusion.2 = f32[100,10,100,10]{3,2,1,0:T(8,128)} fusion(f32[10,10]{1,0:T(8,128)S(1)} %copy-done.8, f32[100,100]{1,0:T(8,128)S(1)} %mul.458), kind=kLoop, calls=%fused_computation.2 | loop fusion | flops 1000000 | bytes 4040400 | tf_op jit(solution)/shard_map/jit(kron)/mul | solution.py:152
  624.8 31.2 %mul.462 = f32[1000,1000]{1,0:T(8,128)} reshape(f32[100,10,100,10]{3,2,1,0:T(8,128)} %broadcast_multiply_fusion.2) | data formatting | bytes 8000000 | tf_op jit(solution)/shard_map/jit(kron)/mul | solution.py:152
  656.0 0.0 copy-start.3
  656.1 0.1 maximum_bitcast_fusion.2
  656.2 0.1 maximum_bitcast_fusion.4
  656.3 1.1 pad_maximum_fusion.1.near
  657.4 1.0 copy-done.2
  658.4 0.9 reduce-precision_convert_fusion.2
  659.4 0.3 copy-done.3
  659.7 0.9 reduce-precision_convert_fusion.1
  660.6 0.0 slice-start
  660.6 4.0 maximum_bitcast_fusion
  664.7 7.5 pad_maximum_fusion.far
  672.1 0.0 slice-done
  672.1 0.0 slice-done.1
  672.1 13.9 %fusion.25 = f32[1000,8,384]{2,0,1:T(8,128)} fusion(bf16[384,8,1000]{0,2,1:T(8,128)(2,1)S(1)} %bitcast.78, f32[1000,1000]{1,0:T(8,128)} %mul.481, f32[1000,1000]{1,0:T(8,128)} %mul.469, f32[1000,1000]{1,0:T(8,128)} %mul.477), kind=kOutput, calls=%fused_computation.47 | convolution fusion | flops 6147999744 | bytes 30432000 | tf_op jit(solution)/shard_map/ij,bjn->bin/dot_general | solution.py:172
  686.1 19.7 %fusion.3 = f32[8,1000,384]{2,1,0:T(8,128)} fusion(f32[8,1000]{1,0:T(8,128)S(1)} %copy-done.6, f32[1000,8,384]{2,0,1:T(8,128)} %get-tuple-element.35, f32[1000,8,384]{2,0,1:T(8,128)} %fusion.18, bf16[8,1000,768]{2,1,0:T(8,128)(2,1)} %all-gather.2.cloned.1.call-done, bf16[384,768]{1,0:T(8,128)(2,1)S(1)} %copy-done), kind=kOutput, calls=%fused_computation.13 | convolution fusion | flops 4727808000 | bytes 49773824 | tf_op jit(solution)/shard_map/bcj,ij->bci/dot_general | solution.py:158
  705.8 13.8 %fusion.12 = f32[8,384,1000]{1,2,0:T(8,128)} fusion(f32[8,1000,384]{2,1,0:T(8,128)} %fusion.3, f32[1000,1000]{1,0:T(8,128)} %mul.462), kind=kOutput, calls=%fused_computation.38 | convolution fusion | flops 6152143872 | bytes 28576000 | tf_op jit(solution)/shard_map/ij,bjn->bin/dot_general | solution.py:164
  719.6 0.0 copy-done.1
  719.6 0.7 copy-done.4
  720.3 9.2 %fusion.11 = f32[8,384,1000]{1,2,0:T(8,128)} fusion(f32[8,1000,384]{2,1,0:T(8,128)S(1)} %copy-done.1, f32[1000,1000]{1,0:T(8,128)S(1)} %copy-done.4), kind=kOutput, calls=%fused_computation.37 | convolution fusion | flops 6153143808 | bytes 28576000 | tf_op jit(solution)/shard_map/ij,bjn->bin/dot_general | solution.py:164
  729.4 9.5 %fusion.4 = f32[8,384,1000]{1,2,0:T(8,128)} fusion(f32[8,1000,384]{2,1,0:T(8,128)S(1)} %copy-done.1, f32[1000,1000]{1,0:T(8,128)S(1)} %copy-done.4), kind=kOutput, calls=%fused_computation.15 | convolution fusion | flops 6155215872 | bytes 28576000 | tf_op jit(solution)/shard_map/ij,bjn->bin/dot_general | solution.py:164
  739.0 29.5 %bitcast_add_fusion.part = f32[8,1000,384]{2,1,0:T(8,128)} fusion(f32[1000,8,384]{2,0,1:T(8,128)} %fusion.25, f32[8,384,1000]{1,2,0:T(8,128)} %fusion.11, f32[8,384,1000]{1,2,0:T(8,128)} %fusion.12, f32[8,384,1000]{1,2,0:T(8,128)} %fusion.4, bf16[384,8,1000]{0,2,1:T(8,128)(2,1)} %param.11, f32[1000,1000]{1,0:T(8,128)} %mul.481, f32[1000,1000]{1,0:T(8,128)} %mul.469, ...), kind=kOutput, calls=%fused_computation.7 | convolution fusion | flops 6161288192 | bytes 79584000 | tf_op jit(solution)/shard_map/ij,bjn->bin/dot_general | solution.py:172
  768.5 0.0 all-to-all-done.come
  768.5 73.8 %shard_map.110 = bf16[8,1000,384]{2,1,0:T(8,128)(2,1)} custom-call(s32[6,8]{1,0:T(8,128)} %faces.1, s32[1]{0:T(128)S(6)} %copy.15.count, bf16[8,1000,384]{2,1,0:T(8,128)(2,1)} %bitcast.76, bf16[16,1000,384]{2,1,0:T(8,128)(2,1)} %all-to-all-done.come, f32[8,1000,384]{2,1,0:T(8,128)} %bitcast_add_fusion.part, bf16[2,2,1000,1000]{3,2,1,0:T(8,128)(2,1)} %pad_maximum_fusion.far, ...), custom_call_target="tpu_custom_call" | custom-call | tf_op jit(solution)/shard_map/pallas_call | solution.py:107
  (22 shorter events, 0.2 us)
Async XLA Ops:
  6.5 679.5 %copy-start = (bf16[384,768]{1,0:T(8,128)(2,1)S(1)}, bf16[384,768]{1,0:T(8,128)(2,1)}, u32[]{:S(2)}) copy-start(bf16[384,768]{1,0:T(8,128)(2,1)} %param.14) | copy-start | bytes 1769476
  380.8 7.3 copy-start.10
  380.8 7.3 copy-start.7
  380.9 387.6 %all-to-all-start = ((bf16[16,1000,384]{2,1,0:T(8,128)(2,1)}), bf16[16,1000,384]{2,1,0:T(8,128)(2,1)}, u32[]{:S(2)}, u32[]{:S(2)}) async-start(bf16[16,1000,384]{2,1,0:T(8,128)(2,1)} %shard_map.109), calls=%async_computation | async-start | bytes 24576000 | tf_op jit(solution)/shard_map/all_to_all | solution.py:148
  388.1 298.0 %all-gather.2.cloned.1.call-start = ((), (), s32[]{:S(2)}) async-start(), calls=%async_computation.1 | async-start | bytes 18432000 | tf_op jit(solution)/shard_map/all_gather | solution.py:157
  437.2 13.2 %copy-start.5 = (f32[1000,1000]{1,0:T(8,128)S(1)}, f32[1000,1000]{1,0:T(8,128)}, u32[]{:S(2)}) copy-start(f32[1000,1000]{1,0:T(8,128)} %mul.452) | copy-start | bytes 12000004
  466.4 0.7 copy-start.9
  466.4 0.8 copy-start.8
  656.0 2.5 copy-start.2
  656.0 3.7 copy-start.3
  660.6 11.5 %slice-start = ((s8[6144000]{0:T(1024)(128)(4,1)}), s8[4194304]{0:T(1024)(128)(4,1)S(1)}, s32[]{:S(2)}) async-start(s8[6144000]{0:T(1024)(128)(4,1)} %bitcast.77), calls=%async_computation.2 | async-start | bytes 8388608
  664.7 7.5 slice-start.1
  672.1 14.0 %copy-start.6 = (f32[8,1000]{1,0:T(8,128)S(1)}, f32[8,1000]{1,0:T(8,128)}, u32[]{:S(2)}) copy-start(f32[8,1000]{1,0:T(8,128)} %param.13) | copy-start | bytes 96004
  705.8 13.8 %copy-start.1 = (f32[8,1000,384]{2,1,0:T(8,128)S(1)}, f32[8,1000,384]{2,1,0:T(8,128)}, u32[]{:S(2)}) copy-start(f32[8,1000,384]{2,1,0:T(8,128)} %fusion.3) | copy-start | bytes 36864004
  705.8 14.4 %copy-start.4 = (f32[1000,1000]{1,0:T(8,128)S(1)}, f32[1000,1000]{1,0:T(8,128)}, u32[]{:S(2)}) copy-start(f32[1000,1000]{1,0:T(8,128)} %mul.462) | copy-start | bytes 12000004
Sparse Core Ops, SparseCore 0:
  466.5 25.7 all-gather.1
